TPU v7x, 32 devices: a whole 2x2x4 slice. The times are simulated.
32 devices in a mesh: groups: 2 (over y), seq: 4 (over z), head: 2 (over x), rep: 2 (over core).
Axes of the slice: x: 2, y: 2, z: 4, core: 2. Of those that a mesh axis runs over, the one named last changes fastest.
Arguments:
- queries: bfloat16 [8192, 2048], P(('groups', 'seq'), ('head', 'rep')), parts along dimension 0, may hold values from -8 to 8
- keys_values: bfloat16 [2, 8192, 2048], P(None, ('groups', 'seq'), ('head', 'rep')), parts along dimension 1, may hold values from -8 to 8
- pack_pos: int32 [1024], P('groups'), parts along dimension 0, may hold values from 0 to 4095
- bounds: int32 [2, 8192], P(None, ('groups', 'seq')), parts along dimension 1, may hold values from 0 to 4096, as said below
- radius: int32 [32], P(('head', 'rep')), may hold values from 128 to 512, as said below
- pack_proj: bfloat16 [2, 2048, 2048], P(None, None, ('head', 'rep')), may hold values from -0.5 to 0.5
Outputs:
- mixed: bfloat16 [8192, 2048], P(('groups', 'seq'), ('head', 'rep')), parts along dimension 0
There are 2 independent parts, one for each index of `groups`. A program takes and returns all parts, laid end to end along the dimension named above; an argument that names none is the same for every part. Nothing has to cross between parts.
Inputs may be any that keep to these rules, and one draw needn't show every extreme that they name: bounds[0, s] and bounds[1, s] are the first position and the end (exclusive) of the document of token s; the 8 documents are contiguous and tile the sequence. Some head has radius exactly 512.
All inputs are finite; a program needn't handle non-finite values.
Results may differ from a plain program's by a relative error of at most 0.012.
Values may be sent and summed in bfloat16 or wider, within the bound.
A program may use at most 128 MiB of HBM per device.

v0:
```python
import math

import jax
import jax.numpy as jnp
from jax import lax
from jax.sharding import PartitionSpec as P

HEAD_DIM = 64
PACK = 512
RADIUS = 512


def padded(cells, sides, width):
    for axis, dim in sides:
        count = lax.axis_size(axis)
        ends = count - 1
        head = lax.slice_in_dim(cells, 0, width, axis=dim)
        tail = lax.slice_in_dim(cells, cells.shape[dim] - width, cells.shape[dim], axis=dim)
        cells = jnp.concatenate(
            [
                lax.ppermute(tail, axis, [(i, (i + 1) % count) for i in range(ends)]),
                cells,
                lax.ppermute(head, axis, [((i + 1) % count, i) for i in range(ends)]),
            ],
            axis=dim,
        )
    return cells


def divide_heads(summed, totals):
    rows_here, heads_here = totals.shape
    shaped = summed.reshape(rows_here, heads_here, -1) / totals[:, :, None]
    return shaped.reshape(rows_here, -1)


def attend(
    query_block,
    window_keys,
    window_values,
    pack_key_heads,
    pack_value_heads,
    lower,
    upper,
    radius,
    first_pos,
):
    rows_here = query_block.shape[0]
    window_len = window_keys.shape[0]
    scale = 1.0 / math.sqrt(HEAD_DIM)
    pack_scores = (
        jnp.einsum("qhd,phd->hqp", query_block, pack_key_heads, preferred_element_type=jnp.float32)
        * scale
    )
    window_scores = (
        jnp.einsum("qhd,khd->hqk", query_block, window_keys, preferred_element_type=jnp.float32)
        * scale
    )
    query_pos = first_pos + jnp.arange(rows_here, dtype=jnp.int32)
    key_pos = first_pos - RADIUS + jnp.arange(window_len, dtype=jnp.int32)
    distance = jnp.abs(key_pos[None, :] - query_pos[:, None])
    inside = (key_pos[None, :] >= lower[:, None]) & (key_pos[None, :] < upper[:, None])
    allowed = (distance[None, :, :] <= radius[:, None, None]) & inside[None, :, :]
    window_scores = jnp.where(allowed, window_scores, -1e30)
    highest = jnp.maximum(jnp.max(pack_scores, axis=2), jnp.max(window_scores, axis=2))
    pack_weights = jnp.exp(pack_scores - highest[:, :, None])
    window_weights = jnp.exp(window_scores - highest[:, :, None])
    totals = jnp.sum(pack_weights, axis=2) + jnp.sum(window_weights, axis=2)
    summed = jnp.einsum(
        "hqp,phd->qhd",
        pack_weights.astype(jnp.bfloat16),
        pack_value_heads,
        preferred_element_type=jnp.float32,
    )
    summed = summed + jnp.einsum(
        "hqk,khd->qhd",
        window_weights.astype(jnp.bfloat16),
        window_values,
        preferred_element_type=jnp.float32,
    )
    return (summed / totals.T[:, :, None]).reshape(rows_here, -1).astype(jnp.bfloat16)


def shards(queries, keys_values, pack_pos, bounds, radius, pack_proj):
    tokens_here, width = queries.shape
    heads_here = radius.shape[0]
    scale = 1.0 / math.sqrt(HEAD_DIM)
    offset_pos = lax.axis_index("seq") * tokens_here
    local_pos = pack_pos - offset_pos
    selector = (local_pos[:, None] == jnp.arange(tokens_here, dtype=jnp.int32)[None, :]).astype(
        jnp.bfloat16
    )
    picked = jnp.dot(selector, queries, preferred_element_type=jnp.float32)
    picked_share = lax.psum_scatter(
        picked.astype(jnp.bfloat16), "seq", scatter_dimension=0, tiled=True
    )
    pack_query = lax.all_gather(picked_share, "seq", axis=0, tiled=True)
    query_heads = pack_query.reshape(PACK, heads_here, HEAD_DIM)
    key_heads = keys_values[0].reshape(tokens_here, heads_here, HEAD_DIM)
    value_heads = keys_values[1].reshape(tokens_here, heads_here, HEAD_DIM)
    pack_scores = (
        jnp.einsum("phd,thd->pht", query_heads, key_heads, preferred_element_type=jnp.float32)
        * scale
    )
    local_top = jnp.max(pack_scores, axis=2)
    global_top = lax.pmax(local_top, "seq")
    pack_weights = jnp.exp(pack_scores - global_top[:, :, None])
    row_total = jnp.sum(pack_weights, axis=2)
    row_sum = jnp.einsum(
        "pht,thd->phd",
        pack_weights.astype(jnp.bfloat16),
        value_heads,
        preferred_element_type=jnp.float32,
    ).reshape(PACK, width)
    whole_sum, whole_total = lax.psum((row_sum, row_total), "seq")
    packed = divide_heads(whole_sum, whole_total).astype(jnp.bfloat16)
    portion = lax.all_gather(packed, ("head", "rep"), axis=1, tiled=True)
    key_part = jnp.dot(portion, pack_proj[0], preferred_element_type=jnp.float32)
    value_part = jnp.dot(portion, pack_proj[1], preferred_element_type=jnp.float32)
    pack_keys = key_part.astype(jnp.bfloat16)
    pack_values = value_part.astype(jnp.bfloat16)
    extended = padded(keys_values, (("seq", 1),), RADIUS)
    rows_per = math.gcd(tokens_here, 512)
    window_len = rows_per + 2 * RADIUS
    pack_key_heads = pack_keys.reshape(PACK, heads_here, HEAD_DIM)
    pack_value_heads = pack_values.reshape(PACK, heads_here, HEAD_DIM)

    def token_block(which_block):
        offset_row = which_block * rows_per
        query_block = lax.dynamic_slice_in_dim(queries, offset_row, rows_per, 0).reshape(
            rows_per, heads_here, HEAD_DIM
        )
        window = lax.dynamic_slice_in_dim(extended, offset_row, window_len, 1)
        window_keys = window[0].reshape(window_len, heads_here, HEAD_DIM)
        window_values = window[1].reshape(window_len, heads_here, HEAD_DIM)
        lower = lax.dynamic_slice_in_dim(bounds[0], offset_row, rows_per, 0)
        upper = lax.dynamic_slice_in_dim(bounds[1], offset_row, rows_per, 0)
        return attend(
            query_block,
            window_keys,
            window_values,
            pack_key_heads,
            pack_value_heads,
            lower,
            upper,
            radius,
            offset_pos + offset_row,
        )

    blocks_out = lax.map(token_block, jnp.arange(tokens_here // rows_per, dtype=jnp.int32))
    return blocks_out.reshape(tokens_here, width)


def solution(mesh):
    return jax.shard_map(
        shards,
        mesh=mesh,
        in_specs=(
            P(("groups", "seq"), ("head", "rep")),
            P(None, ("groups", "seq"), ("head", "rep")),
            P("groups"),
            P(None, ("groups", "seq")),
            P(("head", "rep")),
            P(None, None, ("head", "rep")),
        ),
        out_specs=P(("groups", "seq"), ("head", "rep")),
        check_vma=False,
    )
```

profile of v0, /device:TPU:18, one launch (start us, length us, event | category | flops | bytes accessed | tf_op | source)
XLA Modules:
  0.0 282.7 jit_solution(12413389611932709694)
XLA Ops:
  7.2 2.8 fusion.35
  10.1 1.7 fusion.48
  12.8 18.3 %reduce-scatter.2.cloned.1.call-done = bf16[128,512]{1,0:T(8,128)(2,1)} async-done(((bf16[512,512]{1,0:T(8,128)(2,1)}), bf16[128,512]{1,0:T(8,128)(2,1)}) %reduce-scatter.2.cloned.1.call-update) | async-done | bytes 131088 | tf_op jit(solution)/shard_map/reduce_scatter | solution.py:93
  31.1 16.1 %all_gather.6 = bf16[512,512]{1,0:T(8,128)(2,1)S(1)} all-gather(bf16[128,512]{1,0:T(8,128)(2,1)} %reduce-scatter.2.cloned.1.call-done), channel_id=1, replica_groups=mesh['groups'=2,'seq'=4,'head'=2,'rep'=2] {'seq'}, dimensions={0}, use_global_device_ids=true | all-gather | bytes 655360 | tf_op jit(solution)/shard_map/all_gather | solution.py:96
  47.4 8.1 %bitcast_reduce_fusion = (f32[512,8]{0,1:T(8,128)S(1)}, f32[8,512,1024]{2,1,0:T(8,128)}) fusion(bf16[512,8,64]{0,2,1:T(8,128)(2,1)S(1)} %bitcast.103, bf16[1024,8,64]{0,2,1:T(8,128)(2,1)S(1)} %bitcast.102), kind=kOutput, calls=%fused_computation.30 | convolution fusion | flops 545255424 | bytes 18366464 | tf_op jit(solution)/shard_map/phd,thd->pht/dot_general | solution.py:101
  55.5 14.7 %pmax.7 = f32[512,8]{0,1:T(8,128)S(1)} all-reduce(f32[512,8]{0,1:T(8,128)S(1)} %get-tuple-element.185), channel_id=1, replica_groups=mesh['groups'=2,'seq'=4,'head'=2,'rep'=2] {'seq'}, use_global_device_ids=true, to_apply=%region_2.0 | all-reduce | flops 4096 | bytes 32768 | tf_op jit(solution)/shard_map/pmax | solution.py:105
  70.2 8.2 %fusion.26 = f32[8,512,64]{1,2,0:T(8,128)} fusion(bf16[1024,8,64]{0,2,1:T(8,128)(2,1)S(1)} %bitcast.100, f32[8,512,1024]{2,1,0:T(8,128)} %get-tuple-element.186, f32[512,8]{0,1:T(8,128)S(1)} %pmax.7), kind=kOutput, calls=%fused_computation.34 | convolution fusion | flops 549453824 | bytes 18890752 | tf_op jit(solution)/shard_map/pht,thd->phd/dot_general | solution.py:108
  78.5 7.6 %fusion.24 = f32[512,8]{0,1:T(8,128)S(1)} fusion(f32[8,512,1024]{2,1,0:T(8,128)} %get-tuple-element.186, f32[512,8]{0,1:T(8,128)S(1)} %pmax.7), kind=kLoop, calls=%fused_computation.32 | loop fusion | flops 12578816 | bytes 16809984 | tf_op jit(solution)/shard_map/reduce_sum | solution.py:107
  86.1 17.1 %psum.15 = f32[512,8]{0,1:T(8,128)S(1)} all-reduce(f32[512,8]{0,1:T(8,128)S(1)} %fusion.24), channel_id=1, replica_groups=mesh['groups'=2,'seq'=4,'head'=2,'rep'=2] {'seq'}, use_global_device_ids=true, to_apply=%region_5.0 | all-reduce | flops 4096 | bytes 32768 | tf_op jit(solution)/shard_map/psum | solution.py:114
  103.2 28.0 %all-reduce.2.cloned.1.call-done = f32[512,512]{0,1:T(8,128)} async-done(((f32[512,512]{0,1:T(8,128)}), f32[512,512]{0,1:T(8,128)}) %all-reduce.2.cloned.1.call-update) | async-done | bytes 1048592 | tf_op jit(solution)/shard_map/psum | solution.py:114
  131.3 2.2 fusion.42
  133.4 3.0 %copy.20 = bf16[2,1024,512]{1,2,0:T(8,128)(2,1)S(1)} copy(bf16[2,1024,512]{2,1,0:T(8,128)(2,1)} %param.9) | data formatting | bytes 4194304 | tf_op args[1]
  137.6 2.9 %collective-permute-start.1 = (bf16[2,512,512]{1,2,0:T(8,128)(2,1)}, bf16[2,512,512]{1,2,0:T(8,128)(2,1)}, u32[]{:S(2)}, u32[]{:S(2)}) collective-permute-start(bf16[2,512,512]{1,2,0:T(8,128)(2,1)} %get-tuple-element.182), channel_id=1, source_target_pairs={{4,0},{8,4},{12,8},{5,1},{9,5},{13,9},{6,2},{10,6},{14,10},{7,3},{... | collective-permute-start | bytes 3145736 | tf_op jit(solution)/shard_map/ppermute | solution.py:23
  140.5 3.9 %collective-permute-start = (bf16[2,512,512]{1,2,0:T(8,128)(2,1)S(1)}, bf16[2,512,512]{1,2,0:T(8,128)(2,1)}, u32[]{:S(2)}, u32[]{:S(2)}) collective-permute-start(bf16[2,512,512]{1,2,0:T(8,128)(2,1)S(1)} %get-tuple-element.181), channel_id=1, source_target_pairs={{0,4},{4,8},{8,12},{1,5},{5,9},{9,13},{2,6},{6,10},{10,14},{3,7},{... | collective-permute-start | bytes 3145736 | tf_op jit(solution)/shard_map/ppermute | solution.py:21
  144.5 20.3 %collective-permute-done.1 = bf16[2,512,512]{1,2,0:T(8,128)(2,1)} collective-permute-done((bf16[2,512,512]{1,2,0:T(8,128)(2,1)}, bf16[2,512,512]{1,2,0:T(8,128)(2,1)}, u32[]{:S(2)}, u32[]{:S(2)}) %collective-permute-start.1) | collective-permute-done | bytes 1048608 | tf_op jit(solution)/shard_map/ppermute | solution.py:23
  164.7 2.2 collective-permute-done
  166.9 3.4 %pad_maximum_fusion = bf16[2,2048,512]{1,2,0:T(8,128)(2,1)} fusion(bf16[2,512,512]{1,2,0:T(8,128)(2,1)} %collective-permute-done.1, bf16[2,1024,512]{1,2,0:T(8,128)(2,1)S(1)} %copy.20, bf16[2,512,512]{1,2,0:T(8,128)(2,1)} %collective-permute-done), kind=kLoop, calls=%fused_computation.35 | loop fusion | flops 12582912 | bytes 8388608 | tf_op jit(solution)/shard_map/concatenate | solution.py:19
  170.3 3.5 %fusion.36 = bf16[512,512]{0,1:T(8,128)(2,1)S(1)} fusion(bf16[512,2048]{0,1:T(8,128)(2,1)} %all-gather.2.cloned.1.call-done, bf16[2,2048,512]{2,1,0:T(8,128)(2,1)} %param.13), kind=kOutput, calls=%fused_computation.45 | convolution fusion | flops 1074003968 | bytes 4718592 | tf_op jit(solution)/shard_map/dot_general | solution.py:117
  173.9 4.3 %fusion.39 = bf16[512,512]{0,1:T(8,128)(2,1)} fusion(bf16[512,2048]{0,1:T(8,128)(2,1)} %all-gather.2.cloned.1.call-done, bf16[2,2048,512]{2,1,0:T(8,128)(2,1)} %param.13), kind=kOutput, calls=%fused_computation.46 | convolution fusion | flops 1074003968 | bytes 4718592 | tf_op jit(solution)/shard_map/dot_general | solution.py:118
  178.2 98.0 %while.12 = (s32[]{:T(128)}, bf16[2,512,512]{2,1,0:T(8,128)(2,1)}, s32[2]{0:T(128)S(1)}, bf16[1024,512]{1,0:T(8,128)(2,1)}, bf16[512,8,64]{0,2,1:T(8,128)(2,1)S(...) while((s32[]{:T(128)}, bf16[2,512,512]{2,1,0:T(8,128)(2,1)}, ...), condition=%wide.region_11.12_spmd, body=%wide.region_6.11_spmd.sunk | while | flops 2225596416 | bytes 137660848 | solution.py:149
  179.8 3.3 %constant_dynamic-slice_fusion.8 = (bf16[1,1536,512]{1,2,0:T(8,128)(2,1)}, bf16[1,1536,512]{1,2,0:T(8,128)(2,1)S(1)}) fusion(bf16[2,2048,512]{1,2,0:T(8,128)(2,1)} %get-tuple-element.310, s32[]{:T(128)S(6)} %select_n.24, s32[]{:T(128)S(6)} %add.106), kind=kLoop, calls=%fused_computation.22.clone.1 | loop fusion | bytes 6291464 | tf_op jit(solution)/shard_map/while/body/eval_jaxpr/slice | solution.py:133
  185.6 14.5 %fusion.83 = (f32[8,512]{1,0:T(8,128)S(1)}, f32[8,512,1536]{2,1,0:T(8,128)}) fusion(bf16[512,8,64]{0,2,1:T(8,128)(2,1)S(1)} %bitcast.95, bf16[1536,8,64]{0,2,1:T(8,128)(2,1)} %bitcast.97, pred[512,1536]{1,0:T(8,128)(4,1)S(1)} %compare_and_fusion.2, s32[8]{0:T(128)S(1)} %get-tuple-element.308, s32[512,1536]{1,0:T(8,128)S(1)} %subtract_abs_fusion.2), kind=kOutput, calls=%fused_computation.53.clone.1 | convolution fusion | flops 836759552 | bytes 31211552 | tf_op jit(solution)/shard_map/while/body/eval_jaxpr/qhd,khd->hqk/dot_general | solution.py:55
  201.4 10.3 %fusion.84 = f32[512,8,64]{0,2,1:T(8,128)S(1)} fusion(bf16[1536,8,64]{0,2,1:T(8,128)(2,1)S(1)} %bitcast.94, f32[8,512,1536]{2,1,0:T(8,128)} %get-tuple-element.264, f32[8,512]{1,0:T(8,128)S(1)} %max.13), kind=kOutput, calls=%fused_computation.16.clone.1 | convolution fusion | flops 817889280 | bytes 27803648 | tf_op jit(solution)/shard_map/while/body/eval_jaxpr/hqk,khd->qhd/dot_general | solution.py:74
  211.7 1.4 fusion.85
  213.1 11.3 %fusion.86 = f32[8,512]{1,0:T(8,128)S(1)} fusion(f32[8,512,1536]{2,1,0:T(8,128)} %get-tuple-element.264, f32[8,512]{1,0:T(8,128)S(1)} %max.13), kind=kLoop, calls=%fused_computation.2.clone.1 | loop fusion | flops 12578816 | bytes 25198592 | tf_op jit(solution)/shard_map/while/body/eval_jaxpr/reduce_sum | solution.py:67
  224.4 1.6 divide_convert_fusion.2
  228.7 3.3 %constant_dynamic-slice_fusion.8 = (bf16[1,1536,512]{1,2,0:T(8,128)(2,1)}, bf16[1,1536,512]{1,2,0:T(8,128)(2,1)S(1)}) fusion(bf16[2,2048,512]{1,2,0:T(8,128)(2,1)} %get-tuple-element.310, s32[]{:T(128)S(6)} %select_n.24, s32[]{:T(128)S(6)} %add.106), kind=kLoop, calls=%fused_computation.22.clone.1 | loop fusion | bytes 6291464 | tf_op jit(solution)/shard_map/while/body/eval_jaxpr/slice | solution.py:133
  234.5 14.5 %fusion.83 = (f32[8,512]{1,0:T(8,128)S(1)}, f32[8,512,1536]{2,1,0:T(8,128)}) fusion(bf16[512,8,64]{0,2,1:T(8,128)(2,1)S(1)} %bitcast.95, bf16[1536,8,64]{0,2,1:T(8,128)(2,1)} %bitcast.97, pred[512,1536]{1,0:T(8,128)(4,1)S(1)} %compare_and_fusion.2, s32[8]{0:T(128)S(1)} %get-tuple-element.308, s32[512,1536]{1,0:T(8,128)S(1)} %subtract_abs_fusion.2), kind=kOutput, calls=%fused_computation.53.clone.1 | convolution fusion | flops 836759552 | bytes 31211552 | tf_op jit(solution)/shard_map/while/body/eval_jaxpr/qhd,khd->hqk/dot_general | solution.py:55
  250.3 10.3 %fusion.84 = f32[512,8,64]{0,2,1:T(8,128)S(1)} fusion(bf16[1536,8,64]{0,2,1:T(8,128)(2,1)S(1)} %bitcast.94, f32[8,512,1536]{2,1,0:T(8,128)} %get-tuple-element.264, f32[8,512]{1,0:T(8,128)S(1)} %max.13), kind=kOutput, calls=%fused_computation.16.clone.1 | convolution fusion | flops 817889280 | bytes 27803648 | tf_op jit(solution)/shard_map/while/body/eval_jaxpr/hqk,khd->qhd/dot_general | solution.py:74
  260.6 1.4 fusion.85
  262.0 11.3 %fusion.86 = f32[8,512]{1,0:T(8,128)S(1)} fusion(f32[8,512,1536]{2,1,0:T(8,128)} %get-tuple-element.264, f32[8,512]{1,0:T(8,128)S(1)} %max.13), kind=kLoop, calls=%fused_computation.2.clone.1 | loop fusion | flops 12578816 | bytes 25198592 | tf_op jit(solution)/shard_map/while/body/eval_jaxpr/reduce_sum | solution.py:67
  273.3 1.6 divide_convert_fusion.2
  (58 shorter events, 14.7 us)
Async XLA Ops:
  6.5 24.6 %reduce-scatter.2.cloned.1.call-start = ((), (), s32[]{:S(2)}) async-start(), calls=%async_computation.1 | async-start | bytes 655360 | tf_op jit(solution)/shard_map/reduce_scatter | solution.py:93
  10.0 121.2 %all-reduce.2.cloned.1.call-start = ((), (), s32[]{:S(2)}) async-start(), calls=%async_computation.2 | async-start | bytes 2097152 | tf_op jit(solution)/shard_map/psum | solution.py:114
  78.4 91.9 %all-gather.2.cloned.1.call-start = ((), (), s32[]{:S(2)}) async-start(), calls=%async_computation.3 | async-start | bytes 2621440 | tf_op jit(solution)/shard_map/all_gather | solution.py:116
  137.6 27.1 %collective-permute-start.1 = (bf16[2,512,512]{1,2,0:T(8,128)(2,1)}, bf16[2,512,512]{1,2,0:T(8,128)(2,1)}, u32[]{:S(2)}, u32[]{:S(2)}) collective-permute-start(bf16[2,512,512]{1,2,0:T(8,128)(2,1)} %get-tuple-element.182), channel_id=1, source_target_pairs={{4,0},{8,4},{12,8},{5,1},{9,5},{13,9},{6,2},{10,6},{14,10},{7,3},{... | collective-permute-start | bytes 3145736 | tf_op jit(solution)/shard_map/ppermute | solution.py:23
  140.5 26.4 %collective-permute-start = (bf16[2,512,512]{1,2,0:T(8,128)(2,1)S(1)}, bf16[2,512,512]{1,2,0:T(8,128)(2,1)}, u32[]{:S(2)}, u32[]{:S(2)}) collective-permute-start(bf16[2,512,512]{1,2,0:T(8,128)(2,1)S(1)} %get-tuple-element.181), channel_id=1, source_target_pairs={{0,4},{4,8},{8,12},{1,5},{5,9},{9,13},{2,6},{6,10},{10,14},{3,7},{... | collective-permute-start | bytes 3145736 | tf_op jit(solution)/shard_map/ppermute | solution.py:21
  170.3 7.9 %copy-start = (s32[2,1024]{1,0:T(2,128)S(1)}, s32[2,1024]{1,0:T(2,128)}, u32[]{:S(2)}) copy-start(s32[2,1024]{1,0:T(2,128)} %param.11) | copy-start | bytes 24580
  170.3 7.9 %copy-start.3 = (s32[8]{0:T(128)S(1)}, s32[8]{0:T(128)}, u32[]{:S(2)}) copy-start(s32[8]{0:T(128)} %param.12) | copy-start | bytes 100
  213.1 11.4 %copy-start.4 = (bf16[512,8,64]{0,2,1:T(8,128)(2,1)S(1)}, bf16[512,8,64]{0,2,1:T(8,128)(2,1)}, u32[]{:S(2)}) copy-start(bf16[512,8,64]{0,2,1:T(8,128)(2,1)} %get-tuple-element.311) | copy-start | bytes 1572868 | tf_op jit(solution)/shard_map/while
  224.4 1.9 copy-start.1
  226.3 1.0 copy-start.2
  262.0 11.4 %copy-start.4 = (bf16[512,8,64]{0,2,1:T(8,128)(2,1)S(1)}, bf16[512,8,64]{0,2,1:T(8,128)(2,1)}, u32[]{:S(2)}) copy-start(bf16[512,8,64]{0,2,1:T(8,128)(2,1)} %get-tuple-element.311) | copy-start | bytes 1572868 | tf_op jit(solution)/shard_map/while
  273.3 1.9 copy-start.1
  275.2 1.0 copy-start.2
Sparse Core Ops, SparseCore 0:
  10.1 20.9 reduce-scatter.1
  78.5 52.6 all-reduce.1
  133.6 21.6 all-gather.1
where the time goes:
time: 285 us; the launch traced here: 283 us
  matrix products  82.2 us (29%)
  waiting for transfers between devices  68.9 us (24%)
  blocking collectives  47.9 us (17%)
  other arithmetic  41.6 us (15%)
  local copies, waits for them, and re-layouts  20.1 us (7%)
  between operations  13.2 us (5%)
  starting transfers between devices  6.89 us (2%)
    dot_general x2, matrix products, attend(): jnp.einsum('qhd,khd->hqk', query_block, window_keys, preferred_element_ty...  28.9 us
    psum x1, waiting for transfers between devices, shards(): whole_sum, whole_total = lax.psum((row_sum, row_total), 'seq')  28 us
    reduce_sum x4, other arithmetic, attend(): totals = jnp.sum(pack_weights, axis=2) + jnp.sum(window_weights, axis=2)  25.4 us
    dot_general x2, matrix products, attend(): jnp.einsum('hqk,khd->qhd', window_weights.astype(jnp.bfloat16), window_va...  20.6 us
    ppermute x1, waiting for transfers between devices, padded(): lax.ppermute(head, axis, [((i + 1) % count, i) for i in range(ends)])  20.3 us
    reduce_scatter x1, waiting for transfers between devices, shards(): lax.psum_scatter(picked.astype(jnp.bfloat16), 'seq', scatter_dimension=0,...  18.3 us
    psum x1, blocking collectives, shards(): whole_sum, whole_total = lax.psum((row_sum, row_total), 'seq')  17.1 us
    all_gather x1, blocking collectives, shards(): pack_query = lax.all_gather(picked_share, 'seq', axis=0, tiled=True)  16.1 us
  transfers between devices with their start and end apart: 5, of which 4 were waited for; matrix products, arithmetic and copies ran while one was open for 6% of the time, Pallas kernels for 0%

commit v1 on v0

v1 whole, which is shorter than its diff:
```python
import functools
import math

import jax
import jax.numpy as jnp
from jax import lax
from jax.experimental import pallas as pl
from jax.experimental.pallas import tpu as pltpu
from jax.sharding import PartitionSpec as P

HEAD_DIM = 64
PACK = 512
RADIUS = 512
PAIR = 2 * HEAD_DIM
ROWS = 256
LOG2E = 1.4426950408889634
FACTOR = LOG2E / math.sqrt(HEAD_DIM)
LOW = -1e30
VMEM = 48 * 1024 * 1024


def lane_half(rows):
    return lax.broadcasted_iota(jnp.int32, (rows, PAIR), 1) // HEAD_DIM


def dot_t(a, b):
    return lax.dot_general(a, b, (((1,), (1,)), ((), ())), preferred_element_type=jnp.float32)


def only_head(x, h):
    return jnp.where(lane_half(x.shape[0]) == h, x, jnp.zeros_like(x))


def with_ones(x, h):
    return jnp.where(lane_half(x.shape[0]) == h, x, jnp.ones_like(x))


def softmax_dot(scores, values):
    top = jnp.max(scores, axis=1, keepdims=True)
    weights = jnp.exp2((scores - top) * FACTOR)
    acc = jnp.dot(weights.astype(jnp.bfloat16), values, preferred_element_type=jnp.float32)
    return top * FACTOR, acc


def merge_heads(tops, accs):
    half = lane_half(accs[0].shape[0])
    summed = jnp.where(half == 0, accs[0], accs[1])
    total = pltpu.roll(jnp.where(half == 0, accs[1], accs[0]), HEAD_DIM, 1)
    top = jnp.where(half == 0, tops[0], tops[1])
    return summed, total, top


def pack_kernel(q_ref, kv_ref, out_ref, lse_ref):
    keys = kv_ref[0]
    values = [with_ones(kv_ref[1], h) for h in range(2)]
    for r in range(0, q_ref.shape[0], ROWS):
        rows = pl.ds(r, ROWS)
        q = q_ref[rows, :]
        tops, accs = [], []
        for h in range(2):
            top, acc = softmax_dot(dot_t(only_head(q, h), keys), values[h])
            tops.append(top)
            accs.append(acc)
        summed, total, top = merge_heads(tops, accs)
        out_ref[rows, :] = (summed / total).astype(jnp.bfloat16)
        lse_ref[rows, :] = top + jnp.log2(total)


def pack_attention(pack_query, keys_values):
    rows, width = pack_query.shape
    tokens = keys_values.shape[1]
    return pl.pallas_call(
        pack_kernel,
        grid=(width // PAIR,),
        in_specs=[
            pl.BlockSpec((rows, PAIR), lambda i: (0, i)),
            pl.BlockSpec((2, tokens, PAIR), lambda i: (0, 0, i)),
        ],
        out_specs=[pl.BlockSpec((rows, PAIR), lambda i: (0, i))] * 2,
        out_shape=[
            jax.ShapeDtypeStruct((rows, width), jnp.bfloat16),
            jax.ShapeDtypeStruct((rows, width), jnp.float32),
        ],
        compiler_params=pltpu.CompilerParams(vmem_limit_bytes=VMEM),
        cost_estimate=pl.CostEstimate(
            flops=16 * rows * tokens * width,
            bytes_accessed=4 * tokens * width + 8 * rows * width,
            transcendentals=rows * tokens * width // HEAD_DIM,
        ),
        name="pack_attention",
    )(pack_query, keys_values)


def window_kernel(
    radius_ref, bounds_ref, q_ref, own_ref, left_ref, right_ref, limits_ref,
    out_ref, lse_ref, keys, values, accs, tops,
):
    tokens = q_ref.shape[0]
    pair = pl.program_id(0)
    for at, ref in ((0, left_ref), (RADIUS, own_ref), (RADIUS + tokens, right_ref)):
        span = pl.ds(at, ref.shape[1])
        keys[span, :] = ref[0]
        for h in range(2):
            values[h, span, :] = with_ones(ref[1], h)

    def block(b, carry):
        first = pl.multiple_of(b * ROWS, ROWS)
        rows = pl.ds(first, ROWS)
        q = q_ref[rows, :]
        position = first + RADIUS + lax.broadcasted_iota(jnp.int32, (ROWS, 1), 0)
        lower = limits_ref[rows, 0:1]
        upper = limits_ref[rows, 1:2]
        for h in range(2):
            radius = radius_ref[2 * pair + h]
            low = jnp.maximum(lower, position - radius)
            high = jnp.minimum(upper, position + radius + 1)
            start = jnp.maximum(bounds_ref[first], first + RADIUS - radius)
            start = jnp.maximum(start, 0) // 128 * 128
            end = jnp.minimum(bounds_ref[tokens + first + ROWS - 1], first + RADIUS + ROWS + radius)
            need = end - start
            masked_q = only_head(q, h)

            def body(width):
                at = pl.multiple_of(jnp.minimum(start, tokens + 2 * RADIUS - width), 128)
                scores = dot_t(masked_q, keys[pl.ds(at, width), :])
                spot = lax.broadcasted_iota(jnp.int32, (ROWS, width), 1)
                allowed = (spot >= low - at) & (spot < high - at)
                top, acc = softmax_dot(
                    jnp.where(allowed, scores, LOW), values[h, pl.ds(at, width), :]
                )
                accs[h] = acc
                tops[h] = jnp.broadcast_to(top, (ROWS, PAIR))

            widest = ROWS + 2 * RADIUS
            widths = [w for w in (512, 640, 768, 896, 1024, 1152) if w < widest] + [widest]
            for index, width in enumerate(widths):
                fits = need <= width if width < widest else need > widths[index - 1]
                if 0 < index and width < widest:
                    fits = fits & (need > widths[index - 1])
                pl.when(fits)(functools.partial(body, width))
        summed, total, top = merge_heads([tops[0], tops[1]], [accs[0], accs[1]])
        out_ref[rows, :] = summed / total
        lse_ref[rows, :] = top + jnp.log2(total)
        return carry

    lax.fori_loop(0, tokens // ROWS, block, 0)


def window_attention(queries, keys_values, left, right, bounds, radius, first_pos):
    tokens, width = queries.shape
    limits = bounds - (first_pos - RADIUS)
    cost = tokens * (ROWS + 2 * RADIUS)
    spec = lambda shape: pl.BlockSpec(shape, lambda i, *_: (0,) * (len(shape) - 1) + (i,))
    return pl.pallas_call(
        window_kernel,
        grid_spec=pltpu.PrefetchScalarGridSpec(
            num_scalar_prefetch=2,
            grid=(width // PAIR,),
            in_specs=[
                spec((tokens, PAIR)),
                spec((2, tokens, PAIR)),
                spec((2, RADIUS, PAIR)),
                spec((2, RADIUS, PAIR)),
                pl.BlockSpec((tokens, 2), lambda i, *_: (0, 0)),
            ],
            out_specs=[spec((tokens, PAIR))] * 2,
            scratch_shapes=[
                pltpu.VMEM((tokens + 2 * RADIUS, PAIR), jnp.bfloat16),
                pltpu.VMEM((2, tokens + 2 * RADIUS, PAIR), jnp.bfloat16),
                pltpu.VMEM((2, ROWS, PAIR), jnp.float32),
                pltpu.VMEM((2, ROWS, PAIR), jnp.float32),
            ],
        ),
        out_shape=[jax.ShapeDtypeStruct((tokens, width), jnp.float32)] * 2,
        compiler_params=pltpu.CompilerParams(vmem_limit_bytes=VMEM),
        cost_estimate=pl.CostEstimate(
            flops=16 * cost * width,
            bytes_accessed=20 * tokens * width,
            transcendentals=cost * width // HEAD_DIM,
        ),
        name="window_attention",
    )(radius, limits.reshape(-1), queries, keys_values, left, right, limits.T)


def final_kernel(q_ref, pack_ref, part_ref, lse_ref, out_ref):
    keys = pack_ref[0]
    values = [with_ones(pack_ref[1], h) for h in range(2)]
    for r in range(0, q_ref.shape[0], ROWS):
        rows = pl.ds(r, ROWS)
        q = q_ref[rows, :]
        tops, accs = [], []
        for h in range(2):
            top, acc = softmax_dot(dot_t(only_head(q, h), keys), values[h])
            tops.append(top)
            accs.append(acc)
        summed, total, top = merge_heads(tops, accs)
        other = lse_ref[rows, :]
        highest = jnp.maximum(top, other)
        mine = jnp.exp2(top - highest)
        theirs = jnp.exp2(other - highest)
        out_ref[rows, :] = (
            (summed * mine + part_ref[rows, :] * theirs) / (total * mine + theirs)
        ).astype(jnp.bfloat16)


def final_attention(queries, pack_kv, part, lse):
    tokens, width = queries.shape
    spec = pl.BlockSpec((tokens, PAIR), lambda i: (0, i))
    return pl.pallas_call(
        final_kernel,
        grid=(width // PAIR,),
        in_specs=[spec, pl.BlockSpec((2, PACK, PAIR), lambda i: (0, 0, i)), spec, spec],
        out_specs=spec,
        out_shape=jax.ShapeDtypeStruct((tokens, width), jnp.bfloat16),
        compiler_params=pltpu.CompilerParams(vmem_limit_bytes=VMEM),
        cost_estimate=pl.CostEstimate(
            flops=16 * tokens * PACK * width,
            bytes_accessed=12 * tokens * width,
            transcendentals=tokens * PACK * width // HEAD_DIM,
        ),
        name="final_attention",
    )(queries, pack_kv, part, lse)


def project_kernel(order_ref, part_ref, proj_ref, out_ref, acc):
    step = pl.program_id(0)

    @pl.when(step == 0)
    def _():
        acc[...] = jnp.zeros_like(acc)

    for which in range(2):
        acc[which] += jnp.dot(part_ref[0], proj_ref[which], preferred_element_type=jnp.float32)

    @pl.when(step == pl.num_programs(0) - 1)
    def _():
        out_ref[...] = acc[...].astype(jnp.bfloat16)


def project(order, parts, pack_proj):
    count, rows, width = parts.shape
    columns = pack_proj.shape[2]
    return pl.pallas_call(
        project_kernel,
        grid_spec=pltpu.PrefetchScalarGridSpec(
            num_scalar_prefetch=1,
            grid=(count,),
            in_specs=[
                pl.BlockSpec((1, rows, width), lambda i, order: (i, 0, 0)),
                pl.BlockSpec((2, width, columns), lambda i, order: (0, order[i], 0)),
            ],
            out_specs=pl.BlockSpec((2, rows, columns), lambda i, order: (0, 0, 0)),
            scratch_shapes=[pltpu.VMEM((2, rows, columns), jnp.float32)],
        ),
        out_shape=jax.ShapeDtypeStruct((2, rows, columns), jnp.bfloat16),
        compiler_params=pltpu.CompilerParams(vmem_limit_bytes=VMEM),
        name="project",
    )(order, parts, pack_proj)


def shifted(x, axis, count, shift):
    return lax.ppermute(x, axis, [(i, (i + shift) % count) for i in range(count)])


def shards(queries, keys_values, pack_pos, bounds, radius, pack_proj):
    tokens, width = queries.shape
    heads = radius.shape[0]
    count = lax.axis_size("seq")
    share = PACK // count
    me = lax.axis_index("seq")
    first_pos = me * tokens

    ahead = (me + jnp.arange(count, dtype=jnp.int32)) % count
    local = pack_pos.reshape(count, share)[ahead].reshape(-1) - first_pos
    selector = (local[:, None] == jnp.arange(tokens, dtype=jnp.int32)[None, :]).astype(jnp.bfloat16)
    picked = jnp.dot(selector, queries, preferred_element_type=jnp.float32).astype(jnp.bfloat16)
    picked = picked.reshape(count, share, width)
    mine = picked[0]
    for s in range(1, count):
        mine = mine + shifted(picked[s], "seq", count, s)
    pack_query = jnp.concatenate([mine] + [shifted(mine, "seq", count, s) for s in range(1, count)])

    ends = count - 1
    left = lax.ppermute(
        keys_values[:, tokens - RADIUS :], "seq", [(i, i + 1) for i in range(ends)]
    )
    right = lax.ppermute(keys_values[:, :RADIUS], "seq", [(i + 1, i) for i in range(ends)])

    part, lse = pack_attention(pack_query, keys_values)
    part = part.reshape(count, share, width)
    lse = lse[:, ::HEAD_DIM].reshape(count, share, heads)
    parts, lses = [part[0]], [lse[0]]
    for s in range(1, count):
        parts.append(shifted(part[count - s], "seq", count, s))
        lses.append(shifted(lse[count - s], "seq", count, s))
    lses = jnp.stack(lses)
    weights = jnp.exp2(lses - jnp.max(lses, axis=0, keepdims=True))
    weights = weights / jnp.sum(weights, axis=0, keepdims=True)
    packed = sum(
        parts[j].astype(jnp.float32).reshape(share, heads, HEAD_DIM) * weights[j][:, :, None]
        for j in range(count)
    )
    packed = packed.reshape(share, width).astype(jnp.bfloat16)

    axes = ("head", "rep")
    sides = lax.axis_size("head") * lax.axis_size("rep")
    here = lax.axis_index("head") * lax.axis_size("rep") + lax.axis_index("rep")
    gathered = jnp.stack([packed] + [shifted(packed, axes, sides, s) for s in range(1, sides)])
    order = (here - jnp.arange(sides, dtype=jnp.int32)) % sides
    pack_share = project(order, gathered, pack_proj)
    pack_kv = jnp.concatenate(
        [pack_share] + [shifted(pack_share, "seq", count, s) for s in range(1, count)], axis=1
    )
    window, window_lse = window_attention(
        queries, keys_values, left, right, bounds, radius, first_pos
    )
    return final_attention(queries, pack_kv, window, window_lse)


def solution(mesh):
    return jax.shard_map(
        shards,
        mesh=mesh,
        in_specs=(
            P(("groups", "seq"), ("head", "rep")),
            P(None, ("groups", "seq"), ("head", "rep")),
            P("groups"),
            P(None, ("groups", "seq")),
            P(("head", "rep")),
            P(None, None, ("head", "rep")),
        ),
        out_specs=P(("groups", "seq"), ("head", "rep")),
        check_vma=False,
    )
```

time: 285 us -> 161 us (0.56)
  matrix products: 82.2 us -> 2.12 us
  Pallas kernels: 0 us -> 58.9 us
  blocking collectives: 47.9 us -> 0 us
  other arithmetic: 41.6 us -> 2.56 us
  starting transfers between devices: 6.89 us -> 30.9 us
  between operations: 13.2 us -> 0.33 us
  local copies, waits for them, and re-layouts: 20.1 us -> 7.48 us
  waiting for transfers between devices: 68.9 us -> 57.2 us
    dot_general x13 -> x1, matrix products: 82.2 us -> 2.12 us  [shards(): jnp.dot(selector, queries, preferred_element_type=jnp.float32)]
    pallas_call x0 -> x4, Pallas kernels: none -> 58.9 us  [the longest x1 34.6 us: window_attention(): pl.pallas_call(window_kernel, grid_spec=pltpu.PrefetchScalarGridSpec(num_...]
    ppermute x2 -> x20, waiting for transfers between devices: 22.5 us -> 57.2 us  [the longest x18 57.2 us: shifted(): lax.ppermute(x, axis, [(i, (i + shift) % count) for i in range(count)])]
    reduce_sum x5 -> x1, other arithmetic: 33 us -> 0.03 us  [shards(): weights = weights / jnp.sum(weights, axis=0, keepdims=True)]
    psum x1 -> x0, waiting for transfers between devices: 28 us -> none  [shards(): whole_sum, whole_total = lax.psum((row_sum, row_total), 'seq')]
    ppermute x2 -> x20, starting transfers between devices: 6.8 us -> 30.9 us  [the longest x18 25 us: shifted(): lax.ppermute(x, axis, [(i, (i + shift) % count) for i in range(count)])]
    reduce_scatter x1 -> x0, waiting for transfers between devices: 18.3 us -> none  [shards(): lax.psum_scatter(picked.astype(jnp.bfloat16), 'seq', scatter_dimension=0,...]
    psum x1 -> x0, blocking collectives: 17.1 us -> none  [shards(): whole_sum, whole_total = lax.psum((row_sum, row_total), 'seq')]
  transfers between devices with their start and end apart: 5 -> 20, of which waited for: 4 -> 12; matrix products, arithmetic and copies ran while one was open for 6% -> 4% of each run, Pallas kernels for 0% -> 7%
where the time goes in v1:
time: 161 us; the launch traced here: 160 us
  Pallas kernels  58.9 us (37%)
  waiting for transfers between devices  57.2 us (36%)
  starting transfers between devices  30.9 us (19%)
  local copies, waits for them, and re-layouts  7.48 us (5%)
  other arithmetic  2.56 us (2%)
  matrix products  2.12 us (1%)
    ppermute x18, waiting for transfers between devices, shifted(): lax.ppermute(x, axis, [(i, (i + shift) % count) for i in range(count)])  57.2 us
    pallas_call x1, Pallas kernels, window_attention(): pl.pallas_call(window_kernel, grid_spec=pltpu.PrefetchScalarGridSpec(num_...  34.6 us
    ppermute x18, starting transfers between devices, shifted(): lax.ppermute(x, axis, [(i, (i + shift) % count) for i in range(count)])  25 us
    pallas_call x1, Pallas kernels, final_attention(): pl.pallas_call(final_kernel, grid=(width // PAIR,), in_specs=[spec, pl.Bl...  13 us
    pallas_call x1, Pallas kernels, pack_attention(): pl.pallas_call(pack_kernel, grid=(width // PAIR,), in_specs=[pl.BlockSpec...  9.06 us
    ppermute x1, starting transfers between devices, shards(): lax.ppermute(keys_values[:, :RADIUS], 'seq', [(i + 1, i) for i in range(e...  3.52 us
  transfers between devices with their start and end apart: 20, of which 12 were waited for; matrix products, arithmetic and copies ran while one was open for 4% of the time, Pallas kernels for 7%

profile of v1, /device:TPU:18, one launch (start us, length us, event | category | flops | bytes accessed | tf_op | source)
XLA Modules:
  0.0 159.6 jit_solution(1029510663411809365)
XLA Ops:
  1.3 2.1 %fusion.1 = bf16[512,512]{1,0:T(8,128)(2,1)S(1)} fusion(bf16[1024,512]{1,0:T(8,128)(2,1)} %q_ref.3, s32[512]{0:T(512)S(1)} %subtract_bitcast_fusion), kind=kOutput, calls=%fused_computation.3 | convolution fusion | flops 537657344 | bytes 1574912 | tf_op jit(solution)/shard_map/dot_general | solution.py:276
  3.4 1.6 %collective-permute-start = (bf16[128,512]{1,0:T(8,128)(2,1)S(1)}, bf16[128,512]{1,0:T(8,128)(2,1)S(1)}, u32[]{:S(2)}, u32[]{:S(2)}) collective-permute-start(bf16[128,512]{1,0:T(8,128)(2,1)S(1)} %get-tuple-element.18), channel_id=1, source_target_pairs={{0,4},{4,8},{8,12},{12,0},{1,5},{5,9},{9,13},{13,1},{2,6},{6,10},{... | collective-permute-start | bytes 393224 | tf_op jit(solution)/shard_map/ppermute | solution.py:262
  5.5 2.1 %collective-permute-start.1 = (bf16[128,512]{1,0:T(8,128)(2,1)S(1)}, bf16[128,512]{1,0:T(8,128)(2,1)S(1)}, u32[]{:S(2)}, u32[]{:S(2)}) collective-permute-start(bf16[128,512]{1,0:T(8,128)(2,1)S(1)} %get-tuple-element.20), channel_id=1, source_target_pairs={{0,8},{4,12},{8,0},{12,4},{1,9},{5,13},{9,1},{13,5},{2,10},{6,14},... | collective-permute-start | bytes 393224 | tf_op jit(solution)/shard_map/ppermute | solution.py:262
  7.6 7.2 %collective-permute-done = bf16[128,512]{1,0:T(8,128)(2,1)S(1)} collective-permute-done((bf16[128,512]{1,0:T(8,128)(2,1)S(1)}, bf16[128,512]{1,0:T(8,128)(2,1)S(1)}, u32[]{:S(2)}, u32[]{:S(2)}) %collective-permute-start) | collective-permute-done | bytes 131104 | tf_op jit(solution)/shard_map/ppermute | solution.py:262
  14.9 1.1 collective-permute-done.1
  16.8 4.3 %collective-permute-start.4 = (bf16[128,512]{1,0:T(8,128)(2,1)S(1)}, bf16[128,512]{1,0:T(8,128)(2,1)S(1)}, u32[]{:S(2)}, u32[]{:S(2)}) collective-permute-start(bf16[128,512]{1,0:T(8,128)(2,1)S(1)} %fusion.4), channel_id=1, source_target_pairs={{0,8},{4,12},{8,0},{12,4},{1,9},{5,13},{9,1},{13,5},{2,10},{6,14},... | collective-permute-start | bytes 393224 | tf_op jit(solution)/shard_map/ppermute | solution.py:262
  21.5 1.5 fusion.11
  22.9 3.5 %collective-permute-start.19 = (bf16[2,512,512]{2,1,0:T(8,128)(2,1)}, bf16[2,512,512]{2,1,0:T(8,128)(2,1)S(1)}, u32[]{:S(2)}, u32[]{:S(2)}) collective-permute-start(bf16[2,512,512]{2,1,0:T(8,128)(2,1)} %get-tuple-element.13), channel_id=1, source_target_pairs={{4,0},{8,4},{12,8},{5,1},{9,5},{13,9},{6,2},{10,6},{14,10},{7,3},{... | collective-permute-start | bytes 3145736 | tf_op jit(solution)/shard_map/ppermute | solution.py:287
  26.4 2.4 %collective-permute-start.18 = (bf16[2,512,512]{2,1,0:T(8,128)(2,1)}, bf16[2,512,512]{2,1,0:T(8,128)(2,1)}, u32[]{:S(2)}, u32[]{:S(2)}) collective-permute-start(bf16[2,512,512]{2,1,0:T(8,128)(2,1)} %get-tuple-element.14), channel_id=1, source_target_pairs={{0,4},{4,8},{8,12},{1,5},{5,9},{9,13},{2,6},{6,10},{10,14},{3,7},{... | collective-permute-start | bytes 3145736 | tf_op jit(solution)/shard_map/ppermute | solution.py:284
  29.5 3.0 %collective-permute-done.3 = bf16[128,512]{1,0:T(8,128)(2,1)S(1)} collective-permute-done((bf16[128,512]{1,0:T(8,128)(2,1)S(1)}, bf16[128,512]{1,0:T(8,128)(2,1)S(1)}, u32[]{:S(2)}, u32[]{:S(2)}) %collective-permute-start.3) | collective-permute-done | bytes 131104 | tf_op jit(solution)/shard_map/ppermute | solution.py:262
  32.6 9.1 %pack_attention.1 = (bf16[512,512]{1,0:T(8,128)(2,1)S(1)}, f32[512,512]{1,0:T(8,128)S(1)}) custom-call(bf16[512,512]{1,0:T(8,128)(2,1)S(1)} %pad_maximum_fusion.1.q_ref, bf16[2,1024,512]{2,1,0:T(8,128)(2,1)S(1)} %copy-done.2), custom_call_target="tpu_custom_call" | custom-call | flops 4294967296 | bytes 4194304 | tf_op jit(solution)/shard_map/pack_attention/pallas_call | solution.py:72
  41.7 1.2 slice.76
  43.0 2.0 %collective-permute-start.8 = (f32[128,8]{1,0:T(8,128)S(1)}, f32[128,8]{1,0:T(8,128)S(1)}, u32[]{:S(2)}, u32[]{:S(2)}) collective-permute-start(f32[128,8]{1,0:T(8,128)S(1)} %get-tuple-element.24), channel_id=1, source_target_pairs={{0,12},{4,0},{8,4},{12,8},{1,13},{5,1},{9,5},{13,9},{2,14},{6,2},{... | collective-permute-start | bytes 12296 | tf_op jit(solution)/shard_map/ppermute | solution.py:262
  45.0 2.2 %collective-permute-start.7 = (f32[128,8]{1,0:T(8,128)S(1)}, f32[128,8]{1,0:T(8,128)S(1)}, u32[]{:S(2)}, u32[]{:S(2)}) collective-permute-start(f32[128,8]{1,0:T(8,128)S(1)} %get-tuple-element.25), channel_id=1, source_target_pairs={{0,8},{4,12},{8,0},{12,4},{1,9},{5,13},{9,1},{13,5},{2,10},{6,14},... | collective-permute-start | bytes 12296 | tf_op jit(solution)/shard_map/ppermute | solution.py:262
  47.2 12.0 %collective-permute-done.6 = f32[128,8]{1,0:T(8,128)S(1)} collective-permute-done((f32[128,8]{1,0:T(8,128)S(1)}, f32[128,8]{1,0:T(8,128)S(1)}, u32[]{:S(2)}, u32[]{:S(2)}) %collective-permute-start.6) | collective-permute-done | bytes 4128 | tf_op jit(solution)/shard_map/ppermute | solution.py:262
  59.2 2.3 %collective-permute-start.11 = (bf16[128,512]{1,0:T(8,128)(2,1)S(1)}, bf16[128,512]{1,0:T(8,128)(2,1)S(1)}, u32[]{:S(2)}, u32[]{:S(2)}) collective-permute-start(bf16[128,512]{1,0:T(8,128)(2,1)S(1)} %get-tuple-element.16), channel_id=1, source_target_pairs={{0,12},{4,0},{8,4},{12,8},{1,13},{5,1},{9,5},{13,9},{2,14},{6,2},{... | collective-permute-start | bytes 393224 | tf_op jit(solution)/shard_map/ppermute | solution.py:262
  61.6 1.8 %collective-permute-start.10 = (bf16[128,512]{1,0:T(8,128)(2,1)S(1)}, bf16[128,512]{1,0:T(8,128)(2,1)}, u32[]{:S(2)}, u32[]{:S(2)}) collective-permute-start(bf16[128,512]{1,0:T(8,128)(2,1)S(1)} %get-tuple-element.17), channel_id=1, source_target_pairs={{0,8},{4,12},{8,0},{12,4},{1,9},{5,13},{9,1},{13,5},{2,10},{6,14},... | collective-permute-start | bytes 393224 | tf_op jit(solution)/shard_map/ppermute | solution.py:262
  64.3 5.6 %collective-permute-done.9 = bf16[128,512]{1,0:T(8,128)(2,1)S(1)} collective-permute-done((bf16[128,512]{1,0:T(8,128)(2,1)S(1)}, bf16[128,512]{1,0:T(8,128)(2,1)S(1)}, u32[]{:S(2)}, u32[]{:S(2)}) %collective-permute-start.9) | collective-permute-done | bytes 131104 | tf_op jit(solution)/shard_map/ppermute | solution.py:262
  69.8 1.1 add_convert_fusion
  72.0 2.8 %collective-permute-done.14 = bf16[128,512]{1,0:T(8,128)(2,1)S(1)} collective-permute-done((bf16[128,512]{1,0:T(8,128)(2,1)S(1)}, bf16[128,512]{1,0:T(8,128)(2,1)S(1)}, u32[]{:S(2)}, u32[]{:S(2)}) %collective-permute-start.14) | collective-permute-done | bytes 131104 | tf_op jit(solution)/shard_map/ppermute | solution.py:262
  74.8 2.9 %collective-permute-done.13 = bf16[128,512]{1,0:T(8,128)(2,1)S(1)} collective-permute-done((bf16[128,512]{1,0:T(8,128)(2,1)S(1)}, bf16[128,512]{1,0:T(8,128)(2,1)S(1)}, u32[]{:S(2)}, u32[]{:S(2)}) %collective-permute-start.13) | collective-permute-done | bytes 131104 | tf_op jit(solution)/shard_map/ppermute | solution.py:262
  77.7 1.0 collective-permute-done.12
  78.8 2.2 %copy-done.1 = bf16[2,2048,512]{2,1,0:T(8,128)(2,1)S(1)} copy-done((bf16[2,2048,512]{2,1,0:T(8,128)(2,1)S(1)}, bf16[2,2048,512]{2,1,0:T(8,128)(2,1)}, u32[]{:S(2)}) %copy-start.1) | copy-done | bytes 4194328
  80.9 2.2 %project.1 = bf16[2,128,512]{2,1,0:T(8,128)(2,1)S(1)} custom-call(s32[4]{0:T(128)S(1)} %and_select_fusion.1.order_ref, bf16[4,128,512]{2,1,0:T(8,128)(2,1)S(1)} %pad_maximum_fusion.2.part_ref, bf16[2,2048,512]{2,1,0:T(8,128)(2,1)S(1)} %copy-done.1), custom_call_target="tpu_custom_call" | custom-call | tf_op jit(solution)/shard_map/project/pallas_call | solution.py:243
  83.2 1.9 %collective-permute-start.17 = (bf16[2,128,512]{2,1,0:T(8,128)(2,1)S(1)}, bf16[2,128,512]{2,1,0:T(8,128)(2,1)}, u32[]{:S(2)}, u32[]{:S(2)}) collective-permute-start(bf16[2,128,512]{2,1,0:T(8,128)(2,1)S(1)} %project.1), channel_id=1, source_target_pairs={{0,12},{4,0},{8,4},{12,8},{1,13},{5,1},{9,5},{13,9},{2,14},{6,2},{... | collective-permute-start | bytes 786440 | tf_op jit(solution)/shard_map/ppermute | solution.py:262
  85.0 4.4 %collective-permute-start.16 = (bf16[2,128,512]{2,1,0:T(8,128)(2,1)S(1)}, bf16[2,128,512]{2,1,0:T(8,128)(2,1)}, u32[]{:S(2)}, u32[]{:S(2)}) collective-permute-start(bf16[2,128,512]{2,1,0:T(8,128)(2,1)S(1)} %project.1), channel_id=1, source_target_pairs={{0,8},{4,12},{8,0},{12,4},{1,9},{5,13},{9,1},{13,5},{2,10},{6,14},... | collective-permute-start | bytes 786440 | tf_op jit(solution)/shard_map/ppermute | solution.py:262
  89.7 4.7 %collective-permute-done.17 = bf16[2,128,512]{2,1,0:T(8,128)(2,1)} collective-permute-done((bf16[2,128,512]{2,1,0:T(8,128)(2,1)S(1)}, bf16[2,128,512]{2,1,0:T(8,128)(2,1)}, u32[]{:S(2)}, u32[]{:S(2)}) %collective-permute-start.17) | collective-permute-done | bytes 262176 | tf_op jit(solution)/shard_map/ppermute | solution.py:262
  94.4 12.1 %collective-permute-done.16 = bf16[2,128,512]{2,1,0:T(8,128)(2,1)} collective-permute-done((bf16[2,128,512]{2,1,0:T(8,128)(2,1)S(1)}, bf16[2,128,512]{2,1,0:T(8,128)(2,1)}, u32[]{:S(2)}, u32[]{:S(2)}) %collective-permute-start.16) | collective-permute-done | bytes 262176 | tf_op jit(solution)/shard_map/ppermute | solution.py:262
  106.5 4.2 %collective-permute-done.15 = bf16[2,128,512]{2,1,0:T(8,128)(2,1)} collective-permute-done((bf16[2,128,512]{2,1,0:T(8,128)(2,1)S(1)}, bf16[2,128,512]{2,1,0:T(8,128)(2,1)}, u32[]{:S(2)}, u32[]{:S(2)}) %collective-permute-start.15) | collective-permute-done | bytes 262176 | tf_op jit(solution)/shard_map/ppermute | solution.py:262
  110.6 1.2 pad_maximum_fusion.pack_ref
  111.9 34.6 %window_attention.1 = (f32[1024,512]{1,0:T(8,128)S(1)}, f32[1024,512]{1,0:T(8,128)}) custom-call(s32[8]{0:T(128)S(1)} %copy-done.4, s32[2048]{0:T(1024)S(1)} %bitcast.34, bf16[1024,512]{1,0:T(8,128)(2,1)S(1)} %copy-done.3, bf16[2,1024,512]{2,1,0:T(8,128)(2,1)} %own_ref.1, bf16[2,512,512]{2,1,0:T(8,128)(2,1)} %collective-permute-done.18.left_ref, ...), custom_call_target="tpu_custom_call" | custom-call | flops 10737418240 | bytes 10485760 | tf_op jit(solution)/shard_map/window_attention/pallas_call | solution.py:154
  146.5 13.0 %final_attention.1 = bf16[1024,512]{1,0:T(8,128)(2,1)} custom-call(bf16[1024,512]{1,0:T(8,128)(2,1)S(1)} %copy-done.3, bf16[2,512,512]{2,1,0:T(8,128)(2,1)S(1)} %pad_maximum_fusion.pack_ref, f32[1024,512]{1,0:T(8,128)S(1)} %get-tuple-element.11.part_ref, f32[1024,512]{1,0:T(8,128)} %get-tuple-element.12.lse_ref), custom_call_target="tpu_custom_call" | custom-call | flops 4294967296 | bytes 6291456 | tf_op jit(solution)/shard_map/final_attention/pallas_call | solution.py:209
  (62 shorter events, 6.2 us)
Async XLA Ops:
  0.0 0.7 copy-start
  1.3 20.2 %copy-start.2 = (bf16[2,1024,512]{2,1,0:T(8,128)(2,1)S(1)}, bf16[2,1024,512]{2,1,0:T(8,128)(2,1)}, u32[]{:S(2)}) copy-start(bf16[2,1024,512]{2,1,0:T(8,128)(2,1)} %own_ref.1) | copy-start | bytes 6291460
  3.4 11.4 %collective-permute-start = (bf16[128,512]{1,0:T(8,128)(2,1)S(1)}, bf16[128,512]{1,0:T(8,128)(2,1)S(1)}, u32[]{:S(2)}, u32[]{:S(2)}) collective-permute-start(bf16[128,512]{1,0:T(8,128)(2,1)S(1)} %get-tuple-element.18), channel_id=1, source_target_pairs={{0,4},{4,8},{8,12},{12,0},{1,5},{5,9},{9,13},{13,1},{2,6},{6,10},{... | collective-permute-start | bytes 393224 | tf_op jit(solution)/shard_map/ppermute | solution.py:262
  5.1 9.8 %collective-permute-start.2 = (bf16[128,512]{1,0:T(8,128)(2,1)S(1)}, bf16[128,512]{1,0:T(8,128)(2,1)S(1)}, u32[]{:S(2)}, u32[]{:S(2)}) collective-permute-start(bf16[128,512]{1,0:T(8,128)(2,1)S(1)} %get-tuple-element.19), channel_id=1, source_target_pairs={{0,12},{4,0},{8,4},{12,8},{1,13},{5,1},{9,5},{13,9},{2,14},{6,2},{... | collective-permute-start | bytes 393224 | tf_op jit(solution)/shard_map/ppermute | solution.py:262
  5.5 10.5 %collective-permute-start.1 = (bf16[128,512]{1,0:T(8,128)(2,1)S(1)}, bf16[128,512]{1,0:T(8,128)(2,1)S(1)}, u32[]{:S(2)}, u32[]{:S(2)}) collective-permute-start(bf16[128,512]{1,0:T(8,128)(2,1)S(1)} %get-tuple-element.20), channel_id=1, source_target_pairs={{0,8},{4,12},{8,0},{12,4},{1,9},{5,13},{9,1},{13,5},{2,10},{6,14},... | collective-permute-start | bytes 393224 | tf_op jit(solution)/shard_map/ppermute | solution.py:262
  16.0 12.8 %collective-permute-start.5 = (bf16[128,512]{1,0:T(8,128)(2,1)S(1)}, bf16[128,512]{1,0:T(8,128)(2,1)S(1)}, u32[]{:S(2)}, u32[]{:S(2)}) collective-permute-start(bf16[128,512]{1,0:T(8,128)(2,1)S(1)} %fusion.4), channel_id=1, source_target_pairs={{0,12},{4,0},{8,4},{12,8},{1,13},{5,1},{9,5},{13,9},{2,14},{6,2},{... | collective-permute-start | bytes 393224 | tf_op jit(solution)/shard_map/ppermute | solution.py:262
  16.8 12.8 %collective-permute-start.4 = (bf16[128,512]{1,0:T(8,128)(2,1)S(1)}, bf16[128,512]{1,0:T(8,128)(2,1)S(1)}, u32[]{:S(2)}, u32[]{:S(2)}) collective-permute-start(bf16[128,512]{1,0:T(8,128)(2,1)S(1)} %fusion.4), channel_id=1, source_target_pairs={{0,8},{4,12},{8,0},{12,4},{1,9},{5,13},{9,1},{13,5},{2,10},{6,14},... | collective-permute-start | bytes 393224 | tf_op jit(solution)/shard_map/ppermute | solution.py:262
  21.1 11.5 %collective-permute-start.3 = (bf16[128,512]{1,0:T(8,128)(2,1)S(1)}, bf16[128,512]{1,0:T(8,128)(2,1)S(1)}, u32[]{:S(2)}, u32[]{:S(2)}) collective-permute-start(bf16[128,512]{1,0:T(8,128)(2,1)S(1)} %fusion.4), channel_id=1, source_target_pairs={{0,4},{4,8},{8,12},{12,0},{1,5},{5,9},{9,13},{13,1},{2,6},{6,10},{... | collective-permute-start | bytes 393224 | tf_op jit(solution)/shard_map/ppermute | solution.py:262
  22.9 88.9 %collective-permute-start.19 = (bf16[2,512,512]{2,1,0:T(8,128)(2,1)}, bf16[2,512,512]{2,1,0:T(8,128)(2,1)S(1)}, u32[]{:S(2)}, u32[]{:S(2)}) collective-permute-start(bf16[2,512,512]{2,1,0:T(8,128)(2,1)} %get-tuple-element.13), channel_id=1, source_target_pairs={{4,0},{8,4},{12,8},{5,1},{9,5},{13,9},{6,2},{10,6},{14,10},{7,3},{... | collective-permute-start | bytes 3145736 | tf_op jit(solution)/shard_map/ppermute | solution.py:287
  26.4 85.4 %collective-permute-start.18 = (bf16[2,512,512]{2,1,0:T(8,128)(2,1)}, bf16[2,512,512]{2,1,0:T(8,128)(2,1)}, u32[]{:S(2)}, u32[]{:S(2)}) collective-permute-start(bf16[2,512,512]{2,1,0:T(8,128)(2,1)} %get-tuple-element.14), channel_id=1, source_target_pairs={{0,4},{4,8},{8,12},{1,5},{5,9},{9,13},{2,6},{6,10},{10,14},{3,7},{... | collective-permute-start | bytes 3145736 | tf_op jit(solution)/shard_map/ppermute | solution.py:284
  42.9 16.3 %collective-permute-start.6 = (f32[128,8]{1,0:T(8,128)S(1)}, f32[128,8]{1,0:T(8,128)S(1)}, u32[]{:S(2)}, u32[]{:S(2)}) collective-permute-start(f32[128,8]{1,0:T(8,128)S(1)} %get-tuple-element.23), channel_id=1, source_target_pairs={{0,4},{4,8},{8,12},{12,0},{1,5},{5,9},{9,13},{13,1},{2,6},{6,10},{... | collective-permute-start | bytes 12296 | tf_op jit(solution)/shard_map/ppermute | solution.py:262
  43.0 16.2 %collective-permute-start.8 = (f32[128,8]{1,0:T(8,128)S(1)}, f32[128,8]{1,0:T(8,128)S(1)}, u32[]{:S(2)}, u32[]{:S(2)}) collective-permute-start(f32[128,8]{1,0:T(8,128)S(1)} %get-tuple-element.24), channel_id=1, source_target_pairs={{0,12},{4,0},{8,4},{12,8},{1,13},{5,1},{9,5},{13,9},{2,14},{6,2},{... | collective-permute-start | bytes 12296 | tf_op jit(solution)/shard_map/ppermute | solution.py:262
  45.0 16.5 %collective-permute-start.7 = (f32[128,8]{1,0:T(8,128)S(1)}, f32[128,8]{1,0:T(8,128)S(1)}, u32[]{:S(2)}, u32[]{:S(2)}) collective-permute-start(f32[128,8]{1,0:T(8,128)S(1)} %get-tuple-element.25), channel_id=1, source_target_pairs={{0,8},{4,12},{8,0},{12,4},{1,9},{5,13},{9,1},{13,5},{2,10},{6,14},... | collective-permute-start | bytes 12296 | tf_op jit(solution)/shard_map/ppermute | solution.py:262
  59.2 10.6 %collective-permute-start.9 = (bf16[128,512]{1,0:T(8,128)(2,1)S(1)}, bf16[128,512]{1,0:T(8,128)(2,1)S(1)}, u32[]{:S(2)}, u32[]{:S(2)}) collective-permute-start(bf16[128,512]{1,0:T(8,128)(2,1)S(1)} %get-tuple-element.15), channel_id=1, source_target_pairs={{0,4},{4,8},{8,12},{12,0},{1,5},{5,9},{9,13},{13,1},{2,6},{6,10},{... | collective-permute-start | bytes 393224 | tf_op jit(solution)/shard_map/ppermute | solution.py:262
  59.2 10.6 %collective-permute-start.11 = (bf16[128,512]{1,0:T(8,128)(2,1)S(1)}, bf16[128,512]{1,0:T(8,128)(2,1)S(1)}, u32[]{:S(2)}, u32[]{:S(2)}) collective-permute-start(bf16[128,512]{1,0:T(8,128)(2,1)S(1)} %get-tuple-element.16), channel_id=1, source_target_pairs={{0,12},{4,0},{8,4},{12,8},{1,13},{5,1},{9,5},{13,9},{2,14},{6,2},{... | collective-permute-start | bytes 393224 | tf_op jit(solution)/shard_map/ppermute | solution.py:262
  61.6 8.3 %collective-permute-start.10 = (bf16[128,512]{1,0:T(8,128)(2,1)S(1)}, bf16[128,512]{1,0:T(8,128)(2,1)}, u32[]{:S(2)}, u32[]{:S(2)}) collective-permute-start(bf16[128,512]{1,0:T(8,128)(2,1)S(1)} %get-tuple-element.17), channel_id=1, source_target_pairs={{0,8},{4,12},{8,0},{12,4},{1,9},{5,13},{9,1},{13,5},{2,10},{6,14},... | collective-permute-start | bytes 393224 | tf_op jit(solution)/shard_map/ppermute | solution.py:262
  63.8 8.0 %copy-start.5 = (s32[2,1024]{1,0:T(2,128)S(1)}, s32[2,1024]{1,0:T(2,128)}, u32[]{:S(2)}) copy-start(s32[2,1024]{1,0:T(2,128)} %param.9) | copy-start | bytes 24580
  70.9 3.9 %collective-permute-start.14 = (bf16[128,512]{1,0:T(8,128)(2,1)S(1)}, bf16[128,512]{1,0:T(8,128)(2,1)S(1)}, u32[]{:S(2)}, u32[]{:S(2)}) collective-permute-start(bf16[128,512]{1,0:T(8,128)(2,1)S(1)} %add_convert_fusion), channel_id=1, source_target_pairs={{0,3},{1,0},{2,1},{3,2},{4,7},{5,4},{6,5},{7,6},{8,11},{9,8},{10,9... | collective-permute-start | bytes 393224 | tf_op jit(solution)/shard_map/ppermute | solution.py:262
  71.0 6.7 %collective-permute-start.13 = (bf16[128,512]{1,0:T(8,128)(2,1)S(1)}, bf16[128,512]{1,0:T(8,128)(2,1)S(1)}, u32[]{:S(2)}, u32[]{:S(2)}) collective-permute-start(bf16[128,512]{1,0:T(8,128)(2,1)S(1)} %add_convert_fusion), channel_id=1, source_target_pairs={{0,2},{1,3},{2,0},{3,1},{4,6},{5,7},{6,4},{7,5},{8,10},{9,11},{10,... | collective-permute-start | bytes 393224 | tf_op jit(solution)/shard_map/ppermute | solution.py:262
  71.6 7.1 %collective-permute-start.12 = (bf16[128,512]{1,0:T(8,128)(2,1)S(1)}, bf16[128,512]{1,0:T(8,128)(2,1)S(1)}, u32[]{:S(2)}, u32[]{:S(2)}) collective-permute-start(bf16[128,512]{1,0:T(8,128)(2,1)S(1)} %add_convert_fusion), channel_id=1, source_target_pairs={{0,1},{1,2},{2,3},{3,0},{4,5},{5,6},{6,7},{7,4},{8,9},{9,10},{10,1... | collective-permute-start | bytes 393224 | tf_op jit(solution)/shard_map/ppermute | solution.py:262
  78.8 2.2 %copy-start.1 = (bf16[2,2048,512]{2,1,0:T(8,128)(2,1)S(1)}, bf16[2,2048,512]{2,1,0:T(8,128)(2,1)}, u32[]{:S(2)}) copy-start(bf16[2,2048,512]{2,1,0:T(8,128)(2,1)} %proj_ref.1) | copy-start | bytes 12582916
  83.2 11.2 %collective-permute-start.17 = (bf16[2,128,512]{2,1,0:T(8,128)(2,1)S(1)}, bf16[2,128,512]{2,1,0:T(8,128)(2,1)}, u32[]{:S(2)}, u32[]{:S(2)}) collective-permute-start(bf16[2,128,512]{2,1,0:T(8,128)(2,1)S(1)} %project.1), channel_id=1, source_target_pairs={{0,12},{4,0},{8,4},{12,8},{1,13},{5,1},{9,5},{13,9},{2,14},{6,2},{... | collective-permute-start | bytes 786440 | tf_op jit(solution)/shard_map/ppermute | solution.py:262
  85.0 21.5 %collective-permute-start.16 = (bf16[2,128,512]{2,1,0:T(8,128)(2,1)S(1)}, bf16[2,128,512]{2,1,0:T(8,128)(2,1)}, u32[]{:S(2)}, u32[]{:S(2)}) collective-permute-start(bf16[2,128,512]{2,1,0:T(8,128)(2,1)S(1)} %project.1), channel_id=1, source_target_pairs={{0,8},{4,12},{8,0},{12,4},{1,9},{5,13},{9,1},{13,5},{2,10},{6,14},... | collective-permute-start | bytes 786440 | tf_op jit(solution)/shard_map/ppermute | solution.py:262
  89.4 21.2 %collective-permute-start.15 = (bf16[2,128,512]{2,1,0:T(8,128)(2,1)S(1)}, bf16[2,128,512]{2,1,0:T(8,128)(2,1)}, u32[]{:S(2)}, u32[]{:S(2)}) collective-permute-start(bf16[2,128,512]{2,1,0:T(8,128)(2,1)S(1)} %project.1), channel_id=1, source_target_pairs={{0,4},{4,8},{8,12},{12,0},{1,5},{5,9},{9,13},{13,1},{2,6},{6,10},{... | collective-permute-start | bytes 786440 | tf_op jit(solution)/shard_map/ppermute | solution.py:262
  89.4 22.4 %copy-start.3 = (bf16[1024,512]{1,0:T(8,128)(2,1)S(1)}, bf16[1024,512]{1,0:T(8,128)(2,1)}, u32[]{:S(2)}) copy-start(bf16[1024,512]{1,0:T(8,128)(2,1)} %q_ref.3) | copy-start | bytes 3145732
  89.5 22.4 %copy-start.4 = (s32[8]{0:T(128)S(1)}, s32[8]{0:T(128)}, u32[]{:S(2)}) copy-start(s32[8]{0:T(128)} %radius_ref.1) | copy-start | bytes 100
